TPU v7x, 256 devices: a whole 4x4x8 slice. The times are simulated.
256 devices in a mesh: frame: 32 (over y, z_hi, core), view: 8 (over z_lo, x).
Axes of the slice: x: 4, y: 4, z: 8 (z_hi: 4, z_lo: 2; z = z_hi * 2 + z_lo), core: 2. Of those that a mesh axis runs over, the one named last changes fastest.
Arguments:
- hidden: bfloat16 [32, 8, 128, 3072], P('frame', 'view'), may hold values from -3 to 3
- queries: bfloat16 [32, 8, 128, 3072], P('frame', 'view'), may hold values from -120 to 120
- view_keys: bfloat16 [32, 8, 128, 3072], P('frame', 'view'), may hold values from -12 to 12
- view_values: bfloat16 [32, 8, 128, 3072], P('frame', 'view'), may hold values from -12 to 12
- ref_keys: bfloat16 [32, 128, 3072], P('frame'), may hold values from -6 to 6
- ref_values: bfloat16 [32, 128, 3072], P('frame'), may hold values from -12 to 12
- temporal_query: bfloat16 [3072, 3072], P(None, 'view'), may hold values from -1.5 to 1.5
- temporal_key: bfloat16 [3072, 3072], P(None, 'view'), may hold values from -1.5 to 1.5
- temporal_value: bfloat16 [3072, 3072], P(None, 'view'), may hold values from -0.109375 to 0.109375
Outputs:
- mixed: bfloat16 [32, 8, 128, 3072], P('frame', 'view')
- temporal_out: bfloat16 [32, 8, 128, 3072], P('frame', None, None, 'view')
All inputs are finite; a program needn't handle non-finite values.
Results may differ from a plain program's by a relative error of at most 0.035.
Values may be sent and summed in bfloat16 or wider, within the bound.
A program may use at most 128 MiB of HBM per device.

v0:
```python
import jax
import jax.numpy as jnp
from jax import lax
from jax.sharding import PartitionSpec as P

HEADS = 24


def project_rows(block, weight):
    flat = block.reshape(-1, block.shape[-1])
    result = jnp.dot(flat, weight, preferred_element_type=jnp.float32).astype(jnp.bfloat16)
    return result.reshape(block.shape[:-1] + (weight.shape[1],))


def on_device(
    hidden,
    queries,
    view_keys,
    view_values,
    ref_keys,
    ref_values,
    temporal_query,
    temporal_key,
    temporal_value,
):
    frames_here, _, pix, width = queries.shape
    head_size = width // HEADS
    factor = head_size ** (-0.5)
    query_heads = queries.reshape(frames_here, pix, HEADS, head_size)

    def score_block(key_rows):
        key_heads = key_rows.reshape(frames_here, -1, HEADS, head_size)
        return (
            jnp.einsum(
                "fqhd,fkhd->fhqk", query_heads, key_heads, preferred_element_type=jnp.float32
            )
            * factor
        )

    ref_scores = score_block(ref_keys)
    keys_all, values_all = (
        lax.all_gather(view_keys, "view", axis=1, tiled=True),
        lax.all_gather(view_values, "view", axis=1, tiled=True),
    )
    scores = jnp.concatenate([score_block(keys_all), ref_scores], axis=-1)
    weights = jax.nn.softmax(scores, axis=-1).astype(jnp.bfloat16)
    value_rows = jnp.concatenate([values_all.reshape(frames_here, -1, width), ref_values], axis=1)
    value_heads = value_rows.reshape(frames_here, -1, HEADS, head_size)
    attn = jnp.einsum("fhqk,fkhd->fqhd", weights, value_heads, preferred_element_type=jnp.float32)
    mixed = (hidden.astype(jnp.float32) + attn.reshape(frames_here, 1, pix, width)).astype(
        jnp.bfloat16
    )
    gathered = lax.all_gather(mixed, "view", axis=1, tiled=True)
    views = gathered.shape[1]
    token_rows = gathered.reshape(frames_here, views * pix, width)
    moved = lax.all_to_all(token_rows, "frame", split_axis=1, concat_axis=0, tiled=True)
    time_q = project_rows(moved, temporal_query)
    time_k = project_rows(moved, temporal_key)
    time_v = project_rows(moved, temporal_value)
    all_frames, columns_here = (time_q.shape[0], time_q.shape[1])
    local_width = time_q.shape[2]
    head_shape = (all_frames, columns_here, local_width // head_size, head_size)
    time_scores = (
        jnp.einsum(
            "fmhd,gmhd->mhfg",
            time_q.reshape(head_shape),
            time_k.reshape(head_shape),
            preferred_element_type=jnp.float32,
        )
        * factor
    )
    time_weights = jax.nn.softmax(time_scores, axis=-1).astype(jnp.bfloat16)
    time_out = jnp.einsum(
        "mhfg,gmhd->fmhd",
        time_weights,
        time_v.reshape(head_shape),
        preferred_element_type=jnp.float32,
    )
    time_out = time_out.reshape(all_frames, columns_here, local_width).astype(jnp.bfloat16)
    returned = lax.all_to_all(time_out, "frame", split_axis=0, concat_axis=1, tiled=True)
    temporal_out = returned.reshape(frames_here, views, pix, local_width)
    return (mixed, temporal_out)


def solution(mesh):
    placed = (
        P("frame", "view", None, None),
        P("frame", "view", None, None),
        P("frame", "view", None, None),
        P("frame", "view", None, None),
        P("frame", None, None),
        P("frame", None, None),
        P(None, "view"),
        P(None, "view"),
        P(None, "view"),
    )
    return jax.shard_map(
        on_device,
        mesh=mesh,
        in_specs=placed,
        out_specs=(P("frame", "view", None, None), P("frame", None, None, "view")),
        check_vma=False,
    )
```

profile of v0, /device:TPU:3, one launch (start us, length us, event | category | flops | bytes accessed | tf_op | source)
XLA Modules:
  0.0 589.3 jit_solution(3827042613580763636)
XLA Ops:
  7.2 0.0 copy-start
  7.2 0.0 all-gather.6.cloned.1.call-start
  7.2 0.7 all-gather.6.cloned.1.call-update
  7.9 0.0 all-gather.4.cloned.1.call-start
  8.0 0.7 all-gather.4.cloned.1.call-update
  8.7 0.0 all-gather.8.cloned.1.call-start
  8.7 1.3 copy.76
  10.0 2.2 copy.78
  12.2 2.3 copy.56
  14.5 3.0 fusion.55
  17.5 67.9 %all-gather.6.cloned.1.call-done = bf16[1,8,128,3072]{3,2,0,1:T(8,128)(2,1)} async-done(((bf16[1,1,128,3072]{3,2,0,1:T(8,128)(2,1)}), bf16[1,8,128,3072]{3,2,0,1:T(8,128)(2,1)}) %all-gather.6.cloned.1.call-update) | async-done | bytes 6291472 | tf_op jit(solution)/shard_map/all_gather | solution.py:42
  85.4 4.7 copy.77
  90.1 5.7 fusion.54
  95.8 65.0 %all-gather.4.cloned.1.call-done = bf16[1,8,128,3072]{3,2,0,1:T(8,128)(2,1)} async-done(((bf16[1,1,128,3072]{3,2,0,1:T(8,128)(2,1)}), bf16[1,8,128,3072]{3,2,0,1:T(8,128)(2,1)}) %all-gather.4.cloned.1.call-update) | async-done | bytes 6291472 | tf_op jit(solution)/shard_map/all_gather | solution.py:43
  160.8 7.3 %copy.75 = bf16[128,8,24,128]{3,2,1,0:T(8,128)(2,1)} copy(bf16[128,8,24,128]{3,1,2,0:T(8,128)(2,1)} %bitcast.68) | data formatting | bytes 12582912
  168.1 9.1 %copy.73 = bf16[1,1024,24,128]{1,3,2,0:T(8,128)(2,1)} copy(bf16[1,1024,24,128]{3,2,1,0:T(8,128)(2,1)} %bitcast.61) | data formatting | bytes 12582912 | tf_op jit(solution)/shard_map/concatenate | solution.py:47
  177.2 0.0 copy-start.1
  177.2 0.0 copy-start.2
  177.2 0.0 copy-start.3
  177.2 7.4 %fusion.4 = f32[24,128]{1,0:T(8,128)S(1)} fusion(f32[1,24,128,128]{3,2,1,0:T(8,128)} %bitcast.70, f32[1,24,128,1024]{3,2,1,0:T(8,128)} %bitcast.58, f32[24,128]{1,0:T(8,128)S(1)} %reduce_max.31), kind=kLoop, calls=%fused_computation.6 | loop fusion | flops 10613760 | bytes 14180352 | tf_op jit(solution)/shard_map/reduce_sum | solution.py:46
  184.6 0.0 copy-done.1
  184.6 0.0 copy-done.2
  184.6 0.1 copy-done.3
  184.7 8.1 %fusion.6 = f32[24,128,128]{2,1,0:T(8,128)} fusion(bf16[1,128,24,128]{1,3,2,0:T(8,128)(2,1)S(1)} %bitcast.79, bf16[1,1024,24,128]{1,3,2,0:T(8,128)(2,1)S(1)} %copy-done.1, f32[24,128,128]{2,1,0:T(8,128)S(1)} %copy-done.2, f32[24,128,1024]{2,1,0:T(8,128)} %get-tuple-element.7, f32[24,128]{1,0:T(8,128)S(1)} %fusion.4, f32[24,128]{1,0:T(8,128)S(1)} %reduce_max.31), kind=kOutput, calls=%fused_computation.9 | convolution fusion | flops 934281216 | bytes 22831104 | tf_op jit(solution)/shard_map/fhqk,fkhd->fqhd/dot_general | solution.py:49
  192.9 3.0 copy.63
  195.9 0.0 copy-done.4
  195.9 2.4 add_convert_fusion
  198.3 0.0 all-gather.8.cloned.1.call-update
  198.4 73.8 %all-gather.8.cloned.1.call-done = bf16[1,8,128,3072]{3,2,0,1:T(8,128)(2,1)} async-done(((bf16[1,1,128,3072]{3,2,0,1:T(8,128)(2,1)}), bf16[1,8,128,3072]{3,2,0,1:T(8,128)(2,1)}) %all-gather.8.cloned.1.call-update) | async-done | bytes 6291472 | tf_op jit(solution)/shard_map/all_gather | solution.py:53
  272.1 12.2 %copy.128 = bf16[1,1024,3072]{2,0,1:T(2,128)(2,1)} copy(bf16[1,1024,3072]{2,1,0:T(8,128)(2,1)} %bitcast.69) | data formatting | bytes 12582912 | tf_op jit(solution)/shard_map/reshape | solution.py:55
  284.3 0.5 broadcast.20
  284.8 37.8 %reduce.7 = bf16[1024,3072]{1,0:T(8,128)(2,1)} reduce(bf16[1024,1,3072]{2,1,0:T(2,128)(2,1)} %bitcast.59, bf16[]{:T(256)} %broadcast.20), dimensions={1}, to_apply=%bitcast.57.reduce_sub_computation | reduce | bytes 12582914
  322.6 12.9 %reshape.137 = bf16[32,2,49152]{2,1,0:T(2,128)(2,1)} reshape(bf16[1024,3072]{1,0:T(8,128)(2,1)} %reduce.7) | data formatting | bytes 12582912
  335.5 151.2 %all_to_all.8 = bf16[32,2,49152]{2,1,0:T(2,128)(2,1)} all-to-all(bf16[32,2,49152]{2,1,0:T(2,128)(2,1)} %reshape.137), channel_id=1, replica_groups=mesh['frame'=32,'view'=8] {'frame'}, dimensions={0} | all-to-all | bytes 12582912 | tf_op jit(solution)/shard_map/all_to_all | solution.py:56
  486.7 21.6 %reshape.138 = bf16[1024,1,3072]{2,1,0:T(2,128)(2,1)} reshape(bf16[32,2,49152]{2,1,0:T(2,128)(2,1)} %all_to_all.8) | data formatting | bytes 12582912
  508.3 0.0 copy-done
  508.3 7.6 %fusion.25 = bf16[1024,384]{1,0:T(8,128)(2,1)} fusion(bf16[3072,384]{1,0:T(8,128)(2,1)S(1)} %copy-done, bf16[1,1024,3072]{2,0,1:T(2,128)(2,1)} %bitcast.62), kind=kOutput, calls=%fused_computation.28 | convolution fusion | flops 2416312320 | bytes 9437184 | tf_op jit(solution)/shard_map/dot_general | solution.py:11
  515.9 2.4 reshape_reshape.10
  518.3 9.5 %fusion.28 = bf16[1024,384]{1,0:T(8,128)(2,1)} fusion(bf16[3072,384]{1,0:T(8,128)(2,1)} %param.16, bf16[1,1024,3072]{2,0,1:T(2,128)(2,1)} %bitcast.63), kind=kOutput, calls=%fused_computation.29 | convolution fusion | flops 2416312320 | bytes 9437184 | tf_op jit(solution)/shard_map/dot_general | solution.py:11
  527.8 3.3 reshape_reshape.11
  531.1 9.5 %fusion.22 = bf16[1024,384]{1,0:T(8,128)(2,1)} fusion(bf16[3072,384]{1,0:T(8,128)(2,1)} %param.17, bf16[1,1024,3072]{2,0,1:T(2,128)(2,1)} %bitcast.64), kind=kOutput, calls=%fused_computation.27 | convolution fusion | flops 2416312320 | bytes 9437184 | tf_op jit(solution)/shard_map/dot_general | solution.py:11
  540.6 3.2 reshape_reshape.9
  543.9 4.1 fusion.56
  547.9 2.6 fusion.31
  550.5 0.5 copy.69
  551.1 1.4 convert_element_type.42
  552.5 29.4 %all_to_all.9 = bf16[32,32,384]{2,1,0:T(8,128)(2,1)S(1)} all-to-all(bf16[32,32,384]{2,1,0:T(8,128)(2,1)} %convert_element_type.42), channel_id=1, replica_groups=mesh['frame'=32,'view'=8] {'frame'}, dimensions={0} | all-to-all | bytes 1572864 | tf_op jit(solution)/shard_map/all_to_all | solution.py:80
  581.9 0.9 copy.130
  (2 shorter events, 0.0 us)
Async XLA Ops:
  7.2 501.2 %copy-start = (bf16[3072,384]{1,0:T(8,128)(2,1)S(1)}, bf16[3072,384]{1,0:T(8,128)(2,1)}, u32[]{:S(2)}) copy-start(bf16[3072,384]{1,0:T(8,128)(2,1)} %param.15) | copy-start | bytes 7077892
  7.2 78.2 %all-gather.6.cloned.1.call-start = ((), (), s32[]{:S(2)}) async-start(), calls=%async_computation.3 | async-start | bytes 7077888 | tf_op jit(solution)/shard_map/all_gather | solution.py:42
  7.9 152.9 %all-gather.4.cloned.1.call-start = ((), (), s32[]{:S(2)}) async-start(), calls=%async_computation.2 | async-start | bytes 7077888 | tf_op jit(solution)/shard_map/all_gather | solution.py:43
  8.7 263.5 %all-gather.8.cloned.1.call-start = ((), (), s32[]{:S(2)}) async-start(), calls=%async_computation.4 | async-start | bytes 7077888 | tf_op jit(solution)/shard_map/all_gather | solution.py:53
  177.2 7.4 %copy-start.1 = (bf16[1,1024,24,128]{1,3,2,0:T(8,128)(2,1)S(1)}, bf16[1,1024,24,128]{1,3,2,0:T(8,128)(2,1)}, u32[]{:S(2)}) copy-start(bf16[1,1024,24,128]{1,3,2,0:T(8,128)(2,1)} %copy.73) | copy-start | bytes 18874372
  177.2 7.4 %copy-start.2 = (f32[24,128,128]{2,1,0:T(8,128)S(1)}, f32[24,128,128]{2,1,0:T(8,128)}, u32[]{:S(2)}) copy-start(f32[24,128,128]{2,1,0:T(8,128)} %get-tuple-element.9) | copy-start | bytes 4718596
  177.2 7.5 %copy-start.3 = (bf16[1,128,3072]{1,2,0:T(8,128)(2,1)S(1)}, bf16[1,128,3072]{1,2,0:T(8,128)(2,1)}, u32[]{:S(2)}) copy-start(bf16[1,128,3072]{1,2,0:T(8,128)(2,1)} %copy.56) | copy-start | bytes 2359300
  184.7 11.2 %copy-start.4 = (bf16[1,1,128,3072]{3,2,1,0:T(8,128)(2,1)S(1)}, bf16[1,1,128,3072]{3,2,1,0:T(8,128)(2,1)}, u32[]{:S(2)}) copy-start(bf16[1,1,128,3072]{3,2,1,0:T(8,128)(2,1)} %param.9) | copy-start | bytes 2359300
Sparse Core Ops, SparseCore 0:
  9.8 75.5 all-gather.5
  87.2 73.5 all-gather.3
  198.5 73.5 all-gather.7
where the time goes:
time: 591 us; the launch traced here: 589 us
  waiting for transfers between devices  208 us (35%)
  blocking collectives  181 us (31%)
  local copies, waits for them, and re-layouts  89 us (15%)
  matrix products  50.2 us (8%)
  other arithmetic  47.6 us (8%)
  between operations  13.8 us (2%)
    all_to_all x1, blocking collectives, on_device(): lax.all_to_all(token_rows, 'frame', split_axis=1, concat_axis=0, tiled=True)  151 us
    all_gather x1, waiting for transfers between devices, on_device(): gathered = lax.all_gather(mixed, 'view', axis=1, tiled=True)  73.8 us
    all_gather x1, waiting for transfers between devices, on_device(): lax.all_gather(view_keys, 'view', axis=1, tiled=True)  67.9 us
    all_gather x1, waiting for transfers between devices, on_device(): lax.all_gather(view_values, 'view', axis=1, tiled=True)  65 us
    unnamed x19, local copies, waits for them, and re-layouts  53.8 us
    unnamed x1, other arithmetic  37.8 us
    all_to_all x1, blocking collectives, on_device(): lax.all_to_all(time_out, 'frame', split_axis=0, concat_axis=1, tiled=True)  29.4 us
    dot_general x3, matrix products, project_rows(): jnp.dot(flat, weight, preferred_element_type=jnp.float32)  26.6 us
  transfers between devices with their start and end apart: 3, of which 3 were waited for; matrix products, arithmetic and copies ran while one was open for 3% of the time, Pallas kernels for 0%

commit v1 on v0

v1 whole, which is shorter than its diff:
```python
import functools

import jax
import jax.numpy as jnp
from jax import lax
from jax.experimental import pallas as pl
from jax.experimental.pallas import tpu as pltpu
from jax.sharding import PartitionSpec as P

MESH = pl.DeviceIdType.MESH
BF16 = jnp.bfloat16
F32 = jnp.float32
SCALE = 128 ** (-0.5) * 1.4426950408889634


def softmax_parts(scores, values):
    top = jnp.max(scores, axis=-1, keepdims=True)
    weights = jnp.exp2((scores - top) * SCALE).astype(BF16)
    product = jnp.dot(weights, values, preferred_element_type=F32)
    return product[:, :128] / product[:, 128:]


def bytes_wait(ref, sem):
    pltpu.make_async_copy(ref, ref, sem).wait()


def kernel(
    hid, qry, key, val, rkey, rval, wq, wk, wv,
    mixed_out, time_out,
    qbuf, kbuf, vbuf, hbuf, abuf, mbuf, xall, wbuf, tqkv, obuf,
    p1_send, p1_recv, loc, h_send, h_recv, wl_sem, w_send, w1_recv, w2_recv, w3_recv,
    p2_send, p2_recv, p3_send, p3_recv, mb_send, mb_recv, p5_send, p5_recv, own_sem,
):
    f = lax.axis_index("frame")
    v = lax.axis_index("view")
    y, zh, c = f // 8, (f // 2) % 4, f % 2
    zl, x = v // 4, v % 4
    z = zh * 2 + zl

    def device(y_, z_, c_, x_):
        return (y_ * 8 + (z_ // 2) * 2 + c_, (z_ % 2) * 4 + x_)

    def column(part, width=384):
        return pl.ds(pl.multiple_of(part * width, width), width)

    def remote(src, dst, send, recv, target):
        return pltpu.make_async_remote_copy(
            src_ref=src, dst_ref=dst, send_sem=send, recv_sem=recv, device_id=target, device_id_type=MESH
        )

    barrier = pltpu.get_barrier_semaphore()

    def greet_same_x(i, _):
        target = device((y + i // 16) % 4, (z + (i // 2) % 8) % 8, (c + i % 2) % 2, x)
        pl.semaphore_signal(barrier, inc=1, device_id=target, device_id_type=MESH)
        return 0

    lax.fori_loop(1, 64, greet_same_x, 0)

    def greet_view(i, _):
        target = (f, (i // 3) * 4 + (x + 1 + i % 3) % 4)
        pl.semaphore_signal(barrier, inc=1, device_id=target, device_id_type=MESH)
        return 0

    lax.fori_loop(0, 6, greet_view, 0)

    def local_heads(h, _):
        cols = pl.ds(pl.multiple_of(v * 384 + h * 128, 128), 128)
        pltpu.make_async_copy(qry.at[:, cols], qbuf.at[h, v], loc.at[h, 0]).start()
        pltpu.make_async_copy(key.at[:, cols], kbuf.at[h, v], loc.at[h, 1]).start()
        pltpu.make_async_copy(rkey.at[:, cols], kbuf.at[h, 8], loc.at[h, 1]).start()
        pltpu.make_async_copy(val.at[:, cols], vbuf.at[h, v, :, 0:128], loc.at[h, 2]).start()
        pltpu.make_async_copy(rval.at[:, cols], vbuf.at[h, 8, :, 0:128], loc.at[h, 2]).start()
        return 0

    lax.fori_loop(0, 3, local_heads, 0)
    pltpu.make_async_copy(hid.at[:, column(v)], hbuf.at[v], own_sem.at[0]).start()

    def load_weights(i, _):
        rows = column(i)
        place = pl.ds(pl.multiple_of((i // 4) * 384, 384), 384)
        for a, w in enumerate((wq, wk, wv)):
            pltpu.make_async_copy(
                w.at[rows], wbuf.at[0, i % 4, place, a * 384 : (a + 1) * 384], wl_sem.at[0]
            ).start()
        return 0

    pl.semaphore_wait(barrier, 69)

    def send_heads(h, _):
        def to(i, _):
            w = (v + i) % 8
            cols = pl.ds(pl.multiple_of(w * 384 + h * 128, 128), 128)
            remote(key.at[:, cols], kbuf.at[h, v], p1_send.at[1], p1_recv.at[h, 1], (f, w)).start()
            remote(qry.at[:, cols], qbuf.at[h, v], p1_send.at[0], p1_recv.at[h, 0], (f, w)).start()
            remote(val.at[:, cols], vbuf.at[h, v, :, 0:128], p1_send.at[2], p1_recv.at[h, 2], (f, w)).start()
            return 0

        return lax.fori_loop(1, 8, to, 0)

    lax.fori_loop(0, 3, send_heads, 0)

    def send_hidden(i, _):
        w = (v + i) % 8
        remote(hid.at[:, column(w)], hbuf.at[v], h_send.at[0], h_recv.at[0], (f, w)).start()
        return 0

    lax.fori_loop(1, 8, send_hidden, 0)

    part = c * 4 + y
    z_far = (z + 7 + 2 * zl) % 8

    def part_place(c_, y_):
        return wbuf.at[1, y_, pl.ds(pl.multiple_of(c_ * 384, 384), 384)]

    for a, w in enumerate((wq, wk, wv)):
        remote(
            w.at[column(part)],
            wbuf.at[1, y, pl.ds(pl.multiple_of(c * 384, 384), 384), a * 384 : (a + 1) * 384],
            w_send.at[0],
            w1_recv.at[0],
            device(y, z_far, c, x),
        ).start()
    lax.fori_loop(0, 8, load_weights, 0)

    vbuf[:, :, :, 128:256] = jnp.ones((3, 9, 128, 128), BF16)

    def view_head(h, _):
        bytes_wait(kbuf.at[h, 0:2], loc.at[h, 1])
        bytes_wait(qbuf.at[h, 0:1], loc.at[h, 0])
        bytes_wait(kbuf.at[h, 0:2], loc.at[h, 2])
        bytes_wait(qbuf.at[h, 0:7], p1_recv.at[h, 0])
        bytes_wait(kbuf.at[h, 0:7], p1_recv.at[h, 1])
        bytes_wait(kbuf.at[h, 0:7], p1_recv.at[h, 2])
        keys = kbuf[h].reshape(1152, 128)
        values = vbuf[h].reshape(1152, 256)

        def rows(r, _):
            q = qbuf[h, pl.ds(r * 2, 2)].reshape(256, 128)
            scores = lax.dot_general(q, keys, (((1,), (1,)), ((), ())), preferred_element_type=F32)
            abuf[h, pl.ds(r * 2, 2)] = softmax_parts(scores, values).reshape(2, 128, 128)
            return 0

        return lax.fori_loop(0, 4, rows, 0)

    lax.fori_loop(0, 2, view_head, 0)

    bytes_wait(part_place(c, y), w1_recv.at[0])
    for i in (1, 3, 2):
        remote(part_place(c, y), part_place(c, y), w_send.at[1], w2_recv.at[0], device((y + i) % 4, z, c, x)).start()

    lax.fori_loop(2, 3, view_head, 0)

    bytes_wait(hbuf.at[0:1], own_sem.at[0])
    bytes_wait(hbuf.at[0:7], h_recv.at[0])

    def tokens_out(d, _):
        y_to = (y + d) % 4
        views = pl.ds(y_to * 2, 2)
        block = hbuf[views].astype(F32) + jnp.concatenate([abuf[h, views] for h in range(3)], axis=-1)
        mbuf[pl.ds(pl.multiple_of(y_to * 256, 256), 256)] = block.reshape(256, 384).astype(BF16)

        def to(j, _):
            z_to, c_to = (z + j // 2) % 8, (c + j % 2) % 2
            group = y_to * 16 + z_to * 2 + c_to
            remote(
                mbuf.at[pl.ds(pl.multiple_of(group * 16, 16), 16)],
                xall.at[x, pl.ds(pl.multiple_of(f * 16, 16), 16), column(zl)],
                p2_send.at[0],
                p2_recv.at[d],
                device(y_to, z_to, c_to, x),
            ).start()
            return 0

        return lax.fori_loop(jnp.where(d == 0, 1, 0), 16, to, 0)

    lax.fori_loop(0, 4, tokens_out, 0)
    mine = pltpu.make_async_copy(
        mbuf.at[pl.ds(pl.multiple_of((y * 16 + z * 2 + c) * 16, 16), 16)],
        xall.at[x, pl.ds(pl.multiple_of(f * 16, 16), 16), column(zl)],
        own_sem.at[1],
    )
    mine.start()
    mine_mixed = pltpu.make_async_copy(
        mbuf.at[pl.ds(pl.multiple_of(v * 128, 128), 128)], mixed_out.at[:, column(v)], own_sem.at[2]
    )
    mine_mixed.start()

    def send_mixed(i, _):
        w = (v + i) % 8
        remote(
            mbuf.at[pl.ds(pl.multiple_of(w * 128, 128), 128)],
            mixed_out.at[:, column(v)],
            mb_send.at[0],
            mb_recv.at[0],
            (f, w),
        ).start()
        return 0

    lax.fori_loop(1, 8, send_mixed, 0)

    def gather(d):
        y_from = (y + 4 - d) % 4
        rows = pl.ds(pl.multiple_of(y_from * 128, 128), 128)
        for i in (1, 3, 2):
            remote(
                xall.at[x, rows], xall.at[x, rows], p3_send.at[0], p3_recv.at[i], (f, zl * 4 + (x + i) % 4)
            ).start()

    mine.wait()
    bytes_wait(mbuf.at[0:240], p2_recv.at[0])
    gather(0)

    def gather_next(d, _):
        bytes_wait(mbuf.at[0:256], p2_recv.at[d])
        gather(d)
        return 0

    lax.fori_loop(1, 4, gather_next, 0)

    bytes_wait(wbuf.at[1, 0:3, 0:384], w2_recv.at[0])
    for i in range(4):
        remote(part_place(c, i), part_place(c, i), w_send.at[2], w3_recv.at[0], device(y, z, 1 - c, x)).start()

    bytes_wait(wbuf.at[0], wl_sem.at[0])
    for i in (1, 3, 2):
        bytes_wait(xall.at[0], p3_recv.at[i])

    row = lax.broadcasted_iota(jnp.int32, (1, 16, 512), 1)
    col = lax.broadcasted_iota(jnp.int32, (1, 16, 512), 2)
    same = row == col % 16
    tqkv[2, :, :, 128:256] = jnp.ones((3, 512, 128), BF16)

    def project(s):
        def rows(r, _):
            at = pl.ds(pl.multiple_of(r * 256, 256), 256)
            total = jnp.dot(xall[0, at], wbuf[s, 0], preferred_element_type=F32)
            for b in range(1, 4):
                total += jnp.dot(xall[b, at], wbuf[s, b], preferred_element_type=F32)
            total = total.astype(BF16)
            for a in range(3):
                for h in range(3):
                    start = a * 384 + h * 128
                    tqkv[a, h, at, 0:128] = total[:, start : start + 128]
            return 0

        lax.fori_loop(0, 2, rows, 0)

    def time_heads(s):
        for h in range(3):
            q, k = tqkv[0, h, :, 0:128], tqkv[1, h, :, 0:128]
            scores = lax.dot_general(q, k, (((1,), (1,)), ((), ())), preferred_element_type=F32)
            scores = jnp.where(same, scores.reshape(32, 16, 512), -jnp.inf).reshape(512, 512)
            obuf[s, :, h * 128 : (h + 1) * 128] = softmax_parts(scores, tqkv[2, h]).astype(BF16)

    group_rows = pl.ds(pl.multiple_of((y * 16 + z * 2 + c) * 16, 16), 16)

    def half(s, _):
        @pl.when(s == 1)
        def _():
            bytes_wait(wbuf.at[1, :, 0:384], w3_recv.at[0])

        project(s)
        time_heads(s)
        zl_to = (zl + s) % 2

        def to(i, _):
            f_to = (f + i) % 32
            remote(
                obuf.at[s, pl.ds(pl.multiple_of(f_to * 16, 16), 16)],
                time_out.at[group_rows],
                p5_send.at[0],
                p5_recv.at[0],
                (f_to, zl_to * 4 + x),
            ).start()
            return 0

        return lax.fori_loop(jnp.where(s == 0, 1, 0), 32, to, 0)

    lax.fori_loop(0, 2, half, 0)
    mine_out = pltpu.make_async_copy(
        obuf.at[0, pl.ds(pl.multiple_of(f * 16, 16), 16)], time_out.at[group_rows], own_sem.at[3]
    )
    mine_out.start()

    mine_mixed.wait()
    mine_out.wait()
    bytes_wait(hbuf.at[0:7], mb_recv.at[0])
    bytes_wait(mbuf.at[0:1008], p5_recv.at[0])
    for a in range(3):
        bytes_wait(kbuf.at[:, 0:7], p1_send.at[a])
    bytes_wait(hbuf.at[0:7], h_send.at[0])
    bytes_wait(wbuf.at[1, 0, 0:384], w_send.at[0])
    bytes_wait(wbuf.at[1, 0:3, 0:384], w_send.at[1])
    bytes_wait(wbuf.at[1, :, 0:384], w_send.at[2])
    bytes_wait(mbuf.at[0:1008], p2_send.at[0])
    bytes_wait(xall.at[0:3], p3_send.at[0])
    bytes_wait(hbuf.at[0:7], mb_send.at[0])
    bytes_wait(mbuf.at[0:1008], p5_send.at[0])


def on_device(hidden, queries, view_keys, view_values, ref_keys, ref_values, temporal_query, temporal_key, temporal_value):
    flat = [a.reshape(128, 3072) for a in (hidden, queries, view_keys, view_values, ref_keys, ref_values)]
    dma = pltpu.SemaphoreType.DMA
    mixed, out = pl.pallas_call(
        kernel,
        out_shape=(jax.ShapeDtypeStruct((128, 3072), BF16), jax.ShapeDtypeStruct((1024, 384), BF16)),
        in_specs=[pl.BlockSpec(memory_space=pl.ANY)] * 9,
        out_specs=(pl.BlockSpec(memory_space=pl.ANY), pl.BlockSpec(memory_space=pl.ANY)),
        scratch_shapes=[
            pltpu.VMEM((3, 8, 128, 128), BF16),
            pltpu.VMEM((3, 9, 128, 128), BF16),
            pltpu.VMEM((3, 9, 128, 256), BF16),
            pltpu.VMEM((8, 128, 384), BF16),
            pltpu.VMEM((3, 8, 128, 128), F32),
            pltpu.VMEM((1024, 384), BF16),
            pltpu.VMEM((4, 512, 768), BF16),
            pltpu.VMEM((2, 4, 768, 1152), BF16),
            pltpu.VMEM((3, 3, 512, 256), BF16),
            pltpu.VMEM((2, 512, 384), BF16),
            dma((3,)), dma((3, 3)), dma((3, 3)), dma((1,)), dma((1,)), dma((1,)), dma((3,)), dma((1,)), dma((1,)), dma((1,)),
            dma((1,)), dma((4,)), dma((1,)), dma((4,)), dma((1,)), dma((1,)), dma((1,)), dma((1,)), dma((4,)),
        ],
        compiler_params=pltpu.CompilerParams(
            collective_id=0, has_side_effects=True, vmem_limit_bytes=58 << 20
        ),
    )(*flat, temporal_query, temporal_key, temporal_value)
    return mixed.reshape(1, 1, 128, 3072), out.reshape(1, 8, 128, 384)


def solution(mesh):
    placed = (
        P("frame", "view", None, None),
        P("frame", "view", None, None),
        P("frame", "view", None, None),
        P("frame", "view", None, None),
        P("frame", None, None),
        P("frame", None, None),
        P(None, "view"),
        P(None, "view"),
        P(None, "view"),
    )
    return jax.shard_map(
        on_device,
        mesh=mesh,
        in_specs=placed,
        out_specs=(P("frame", "view", None, None), P("frame", None, None, "view")),
        check_vma=False,
    )
```

time: 591 us -> 145 us (0.25)
  the two profiles are of different devices: /device:TPU:3 before, /device:TPU:1 now
where the time goes in v1:
time: 145 us
  Pallas kernels  140 us (97%)
  local copies, waits for them, and re-layouts  4.15 us (3%)
    pallas_call x1, Pallas kernels, on_device(): pl.pallas_call(kernel, out_shape=(jax.ShapeDtypeStruct((128, 3072), BF16)...  140 us
    unnamed x2, local copies, waits for them, and re-layouts  4.15 us

profile of v1, /device:TPU:1, one launch (start us, length us, event | category | flops | bytes accessed | tf_op | source)
XLA Modules:
  0.0 144.5 jit_solution(5473091668449832375)
XLA Ops:
  0.6 139.7 %shard_map.104 = (bf16[128,3072]{1,0:T(8,128)(2,1)}, bf16[1024,384]{1,0:T(8,128)(2,1)}) custom-call(bf16[128,3072]{1,0:T(8,128)(2,1)} %bitcast.8, bf16[128,3072]{1,0:T(8,128)(2,1)} %bitcast.9, bf16[128,3072]{1,0:T(8,128)(2,1)} %bitcast.10, bf16[128,3072]{1,0:T(8,128)(2,1)} %bitcast.11, bf16[128,3072]{1,0:T(8,128)(2,1)} %bitcast.12, ...), custom_call_target="tpu_custom_call" | custom-call | tf_op jit(solution)/shard_map/pallas_call | solution.py:305
  140.4 2.1 %copy.13 = bf16[1,1,128,3072]{3,2,1,0:T(8,128)(2,1)} copy(bf16[1,1,128,3072]{3,2,1,0:T(8,128)(2,1)} %bitcast.15) | data formatting | bytes 1572864
  142.5 2.1 %copy.14 = bf16[1,8,128,384]{3,2,1,0:T(8,128)(2,1)} copy(bf16[1,8,128,384]{3,2,1,0:T(8,128)(2,1)} %bitcast.14) | data formatting | bytes 1572864

commit v2 on v1

--- a/solution.py
+++ b/solution.py
@@ -30,12 +30,14 @@
     qbuf, kbuf, vbuf, hbuf, abuf, mbuf, xall, wbuf, tqkv, obuf,
     p1_send, p1_recv, loc, h_send, h_recv, wl_sem, w_send, w1_recv, w2_recv, w3_recv,
     p2_send, p2_recv, p3_send, p3_recv, mb_send, mb_recv, p5_send, p5_recv, own_sem,
+    core_in, plane_in,
 ):
     f = lax.axis_index("frame")
     v = lax.axis_index("view")
     y, zh, c = f // 8, (f // 2) % 4, f % 2
     zl, x = v // 4, v % 4
     z = zh * 2 + zl
+    z_skip = 1 + 6 * zl
 
     def device(y_, z_, c_, x_):
         return (y_ * 8 + (z_ // 2) * 2 + c_, (z_ % 2) * 4 + x_)
@@ -50,19 +52,25 @@
 
     barrier = pltpu.get_barrier_semaphore()
 
-    def greet_same_x(i, _):
-        target = device((y + i // 16) % 4, (z + (i // 2) % 8) % 8, (c + i % 2) % 2, x)
-        pl.semaphore_signal(barrier, inc=1, device_id=target, device_id_type=MESH)
-        return 0
-
-    lax.fori_loop(1, 64, greet_same_x, 0)
+    def greet(target, sem=barrier):
+        pl.semaphore_signal(sem, inc=1, device_id=target, device_id_type=MESH)
 
     def greet_view(i, _):
-        target = (f, (i // 3) * 4 + (x + 1 + i % 3) % 4)
-        pl.semaphore_signal(barrier, inc=1, device_id=target, device_id_type=MESH)
-        return 0
-
-    lax.fori_loop(0, 6, greet_view, 0)
+        greet((f, (v + i) % 8))
+        return 0
+
+    def greet_z(i, _):
+        greet(device(y, (z + i) % 8, c, x))
+        return 0
+
+    def greet_y(i, _):
+        greet(device((y + i) % 4, z, c, x))
+        return 0
+
+    lax.fori_loop(1, 8, greet_view, 0)
+    lax.fori_loop(1, 7, lambda i, _: greet_z(i + jnp.where(i >= z_skip, 1, 0), _), 0)
+    lax.fori_loop(1, 4, greet_y, 0)
+    greet(device(y, z, 1 - c, x))
 
     def local_heads(h, _):
         cols = pl.ds(pl.multiple_of(v * 384 + h * 128, 128), 128)
@@ -85,7 +93,39 @@
             ).start()
         return 0
 
-    pl.semaphore_wait(barrier, 69)
+    pl.semaphore_wait(barrier, 17)
+
+    z_far = (z + 7 + 2 * zl) % 8
+
+    def part_rows(odd, p):
+        block = odd * 4 + p
+        return column(block), wbuf.at[1, p, pl.ds(pl.multiple_of(odd * 384, 384), 384)]
+
+    odd = y % 2
+
+    def bring(n):
+        rows, place = part_rows(odd, 2 * n + c)
+        for a, w in enumerate((wq, wk, wv)):
+            remote(
+                w.at[rows],
+                place.at[:, a * 384 : (a + 1) * 384],
+                w_send.at[0],
+                w1_recv.at[n],
+                device(y, z_far, c, x),
+            ).start()
+
+    def part_wait(sem):
+        bytes_wait(wbuf.at[1, 0, 0:384], sem)
+
+    def to_y(n):
+        _, place = part_rows(odd, 2 * n + c)
+        remote(place, place, w_send.at[1], w2_recv.at[n], device((y + 1 + 2 * n) % 4, z, c, x)).start()
+
+    def to_core(set_odd, n):
+        _, place = part_rows(set_odd, 2 * n + c)
+        remote(place, place, w_send.at[2], w3_recv.at[0], device(y, z, 1 - c, x)).start()
+
+    bring(0)
 
     def send_heads(h, _):
         def to(i, _):
@@ -107,23 +147,11 @@
 
     lax.fori_loop(1, 8, send_hidden, 0)
 
-    part = c * 4 + y
-    z_far = (z + 7 + 2 * zl) % 8
-
-    def part_place(c_, y_):
-        return wbuf.at[1, y_, pl.ds(pl.multiple_of(c_ * 384, 384), 384)]
-
-    for a, w in enumerate((wq, wk, wv)):
-        remote(
-            w.at[column(part)],
-            wbuf.at[1, y, pl.ds(pl.multiple_of(c * 384, 384), 384), a * 384 : (a + 1) * 384],
-            w_send.at[0],
-            w1_recv.at[0],
-            device(y, z_far, c, x),
-        ).start()
+    greet(device(y, z, 1 - c, x), core_in.at[0])
     lax.fori_loop(0, 8, load_weights, 0)
 
     vbuf[:, :, :, 128:256] = jnp.ones((3, 9, 128, 128), BF16)
+    tqkv[:, 2, :, :, 128:256] = jnp.ones((2, 3, 512, 128), BF16)
 
     def view_head(h, _):
         bytes_wait(kbuf.at[h, 0:2], loc.at[h, 1])
@@ -143,41 +171,49 @@
 
         return lax.fori_loop(0, 4, rows, 0)
 
-    lax.fori_loop(0, 2, view_head, 0)
-
-    bytes_wait(part_place(c, y), w1_recv.at[0])
-    for i in (1, 3, 2):
-        remote(part_place(c, y), part_place(c, y), w_send.at[1], w2_recv.at[0], device((y + i) % 4, z, c, x)).start()
-
+    lax.fori_loop(0, 1, view_head, 0)
+    bring(1)
+    pl.semaphore_wait(core_in.at[0], 1)
+    for i in range(1, 4):
+        greet(device((y + i) % 4, z, c, x), plane_in.at[0])
+    lax.fori_loop(1, 2, view_head, 0)
+    part_wait(w1_recv.at[0])
+    to_y(0)
+    to_core(odd, 0)
     lax.fori_loop(2, 3, view_head, 0)
+    pl.semaphore_wait(plane_in.at[0], 3)
 
     bytes_wait(hbuf.at[0:1], own_sem.at[0])
     bytes_wait(hbuf.at[0:7], h_recv.at[0])
 
-    def tokens_out(d, _):
+    def tokens_out(n, _):
+        c_to, d = n // 4, n % 4
         y_to = (y + d) % 4
-        views = pl.ds(y_to * 2, 2)
-        block = hbuf[views].astype(F32) + jnp.concatenate([abuf[h, views] for h in range(3)], axis=-1)
-        mbuf[pl.ds(pl.multiple_of(y_to * 256, 256), 256)] = block.reshape(256, 384).astype(BF16)
+
+        @pl.when(c_to == 0)
+        def _():
+            views = pl.ds(y_to * 2, 2)
+            block = hbuf[views].astype(F32) + jnp.concatenate([abuf[h, views] for h in range(3)], axis=-1)
+            mbuf[pl.ds(pl.multiple_of(y_to * 256, 256), 256)] = block.reshape(256, 384).astype(BF16)
 
         def to(j, _):
-            z_to, c_to = (z + j // 2) % 8, (c + j % 2) % 2
+            z_to = (z + j) % 8
             group = y_to * 16 + z_to * 2 + c_to
             remote(
                 mbuf.at[pl.ds(pl.multiple_of(group * 16, 16), 16)],
-                xall.at[x, pl.ds(pl.multiple_of(f * 16, 16), 16), column(zl)],
+                xall.at[x, pl.ds(pl.multiple_of(d * 128 + (f % 8) * 16, 16), 16), column(zl)],
                 p2_send.at[0],
                 p2_recv.at[d],
                 device(y_to, z_to, c_to, x),
             ).start()
             return 0
 
-        return lax.fori_loop(jnp.where(d == 0, 1, 0), 16, to, 0)
-
-    lax.fori_loop(0, 4, tokens_out, 0)
+        return lax.fori_loop(jnp.where((d == 0) & (c_to == c), 1, 0), 8, to, 0)
+
+    lax.fori_loop(0, 8, tokens_out, 0)
     mine = pltpu.make_async_copy(
         mbuf.at[pl.ds(pl.multiple_of((y * 16 + z * 2 + c) * 16, 16), 16)],
-        xall.at[x, pl.ds(pl.multiple_of(f * 16, 16), 16), column(zl)],
+        xall.at[x, pl.ds(pl.multiple_of((f % 8) * 16, 16), 16), column(zl)],
         own_sem.at[1],
     )
     mine.start()
@@ -187,7 +223,7 @@
     mine_mixed.start()
 
     def send_mixed(i, _):
-        w = (v + i) % 8
+        w = (zl + i // 4) % 2 * 4 + (x + i % 4) % 4
         remote(
             mbuf.at[pl.ds(pl.multiple_of(w * 128, 128), 128)],
             mixed_out.at[:, column(v)],
@@ -197,77 +233,86 @@
         ).start()
         return 0
 
-    lax.fori_loop(1, 8, send_mixed, 0)
-
-    def gather(d):
-        y_from = (y + 4 - d) % 4
-        rows = pl.ds(pl.multiple_of(y_from * 128, 128), 128)
-        for i in (1, 3, 2):
-            remote(
-                xall.at[x, rows], xall.at[x, rows], p3_send.at[0], p3_recv.at[i], (f, zl * 4 + (x + i) % 4)
-            ).start()
+    lax.fori_loop(1, 4, send_mixed, 0)
+    part_wait(w1_recv.at[1])
+    to_y(1)
+    to_core(odd, 1)
+
+    def x_device(i):
+        return (f, zl * 4 + (x + i) % 4)
+
+    def direct(d):
+        rows = pl.ds(pl.multiple_of(d * 128, 128), 128)
+        remote(xall.at[x, rows], xall.at[x, rows], p3_send.at[0], p3_recv.at[0, d], x_device(1)).start()
+        remote(xall.at[x, rows], xall.at[x, rows], p3_send.at[0], p3_recv.at[1, d], x_device(3)).start()
+
+    def forward(d):
+        for n in range(2):
+            bytes_wait(xall.at[0, 0:128], p3_recv.at[n, d])
+            rows = pl.ds(pl.multiple_of(d * 128 + n * 64, 64), 64)
+            block = xall.at[(x + 3 + 2 * n) % 4, rows]
+            remote(block, block, p3_send.at[1], p3_recv.at[2, d], x_device(1 + 2 * n)).start()
+
+    def gather(d, _):
+        bytes_wait(mbuf.at[0:256], p2_recv.at[d])
+        direct(d)
+        forward(d - 1)
+        return 0
 
     mine.wait()
     bytes_wait(mbuf.at[0:240], p2_recv.at[0])
-    gather(0)
-
-    def gather_next(d, _):
-        bytes_wait(mbuf.at[0:256], p2_recv.at[d])
-        gather(d)
-        return 0
-
-    lax.fori_loop(1, 4, gather_next, 0)
-
-    bytes_wait(wbuf.at[1, 0:3, 0:384], w2_recv.at[0])
-    for i in range(4):
-        remote(part_place(c, i), part_place(c, i), w_send.at[2], w3_recv.at[0], device(y, z, 1 - c, x)).start()
-
+    direct(0)
+    lax.fori_loop(1, 2, gather, 0)
+    part_wait(w2_recv.at[0])
+    to_core(1 - odd, 0)
+    lax.fori_loop(2, 4, gather, 0)
     bytes_wait(wbuf.at[0], wl_sem.at[0])
-    for i in (1, 3, 2):
-        bytes_wait(xall.at[0], p3_recv.at[i])
 
     row = lax.broadcasted_iota(jnp.int32, (1, 16, 512), 1)
     col = lax.broadcasted_iota(jnp.int32, (1, 16, 512), 2)
     same = row == col % 16
-    tqkv[2, :, :, 128:256] = jnp.ones((3, 512, 128), BF16)
-
-    def project(s):
-        def rows(r, _):
-            at = pl.ds(pl.multiple_of(r * 256, 256), 256)
-            total = jnp.dot(xall[0, at], wbuf[s, 0], preferred_element_type=F32)
-            for b in range(1, 4):
-                total += jnp.dot(xall[b, at], wbuf[s, b], preferred_element_type=F32)
-            total = total.astype(BF16)
-            for a in range(3):
-                for h in range(3):
-                    start = a * 384 + h * 128
-                    tqkv[a, h, at, 0:128] = total[:, start : start + 128]
-            return 0
-
-        lax.fori_loop(0, 2, rows, 0)
+
+    def project(s, r):
+        at = pl.ds(pl.multiple_of(r * 256, 256), 256)
+        total = jnp.dot(xall[0, at], wbuf[s, 0], preferred_element_type=F32)
+        for b in range(1, 4):
+            total += jnp.dot(xall[b, at], wbuf[s, b], preferred_element_type=F32)
+        total = total.astype(BF16)
+        for a in range(3):
+            for h in range(3):
+                start = a * 384 + h * 128
+                tqkv[s, a, h, at, 0:128] = total[:, start : start + 128]
 
     def time_heads(s):
         for h in range(3):
-            q, k = tqkv[0, h, :, 0:128], tqkv[1, h, :, 0:128]
+            q, k = tqkv[s, 0, h, :, 0:128], tqkv[s, 1, h, :, 0:128]
             scores = lax.dot_general(q, k, (((1,), (1,)), ((), ())), preferred_element_type=F32)
             scores = jnp.where(same, scores.reshape(32, 16, 512), -jnp.inf).reshape(512, 512)
-            obuf[s, :, h * 128 : (h + 1) * 128] = softmax_parts(scores, tqkv[2, h]).astype(BF16)
+            obuf[s, :, h * 128 : (h + 1) * 128] = softmax_parts(scores, tqkv[s, 2, h]).astype(BF16)
 
     group_rows = pl.ds(pl.multiple_of((y * 16 + z * 2 + c) * 16, 16), 16)
 
+    for d in range(2):
+        bytes_wait(xall.at[0, 0:128], p3_recv.at[2, d])
+    project(0, 0)
+    forward(3)
+    part_wait(w2_recv.at[1])
+    to_core(1 - odd, 1)
+    lax.fori_loop(4, 8, send_mixed, 0)
+    bytes_wait(wbuf.at[1, :, 0:384], w3_recv.at[0])
+    project(1, 0)
+    for d in range(2, 4):
+        bytes_wait(xall.at[0, 0:128], p3_recv.at[2, d])
+
     def half(s, _):
-        @pl.when(s == 1)
-        def _():
-            bytes_wait(wbuf.at[1, :, 0:384], w3_recv.at[0])
-
-        project(s)
+        project(s, 1)
         time_heads(s)
         zl_to = (zl + s) % 2
 
         def to(i, _):
             f_to = (f + i) % 32
             remote(
-                obuf.at[s, pl.ds(pl.multiple_of(f_to * 16, 16), 16)],
+                obuf.at[s, pl.ds(pl.multiple_of((y + 4 - f_to // 8) % 4 * 128 + (f_to % 8) * 16, 16), 16)],
                 time_out.at[group_rows],
                 p5_send.at[0],
                 p5_recv.at[0],
@@ -279,7 +324,7 @@
 
     lax.fori_loop(0, 2, half, 0)
     mine_out = pltpu.make_async_copy(
-        obuf.at[0, pl.ds(pl.multiple_of(f * 16, 16), 16)], time_out.at[group_rows], own_sem.at[3]
+        obuf.at[0, pl.ds(pl.multiple_of((f % 8) * 16, 16), 16)], time_out.at[group_rows], own_sem.at[3]
     )
     mine_out.start()
 
@@ -290,13 +335,51 @@
     for a in range(3):
         bytes_wait(kbuf.at[:, 0:7], p1_send.at[a])
     bytes_wait(hbuf.at[0:7], h_send.at[0])
-    bytes_wait(wbuf.at[1, 0, 0:384], w_send.at[0])
-    bytes_wait(wbuf.at[1, 0:3, 0:384], w_send.at[1])
+    bytes_wait(wbuf.at[1, 0:2, 0:384], w_send.at[0])
+    bytes_wait(wbuf.at[1, 0:2, 0:384], w_send.at[1])
     bytes_wait(wbuf.at[1, :, 0:384], w_send.at[2])
     bytes_wait(mbuf.at[0:1008], p2_send.at[0])
-    bytes_wait(xall.at[0:3], p3_send.at[0])
+    bytes_wait(xall.at[0:2], p3_send.at[0])
+    bytes_wait(xall.at[0], p3_send.at[1])
     bytes_wait(hbuf.at[0:7], mb_send.at[0])
     bytes_wait(mbuf.at[0:1008], p5_send.at[0])
+
+
+def copy_kernel(mixed, out, mixed_to, out_to, mixed_held, out_held, sem):
+    steps = []
+    for i in range(4):
+        for n, (src, held, dst, rows) in enumerate(
+            ((mixed, mixed_held, mixed_to, pl.ds(i * 32, 32)), (out, out_held, out_to, pl.ds(i * 256, 256)))
+        ):
+            steps.append(
+                (
+                    pltpu.make_async_copy(src.at[rows], held.at[rows], sem.at[0, n, i]),
+                    pltpu.make_async_copy(held.at[rows], dst.at[rows], sem.at[1, n, i]),
+                )
+            )
+    for read, _ in steps:
+        read.start()
+    for read, write in steps:
+        read.wait()
+        write.start()
+    for _, write in steps:
+        write.wait()
+
+
+def copy_out(mixed, out):
+    anywhere = pl.BlockSpec(memory_space=pl.ANY)
+    return pl.pallas_call(
+        copy_kernel,
+        out_shape=(jax.ShapeDtypeStruct(mixed.shape, mixed.dtype), jax.ShapeDtypeStruct(out.shape, out.dtype)),
+        in_specs=[anywhere] * 2,
+        out_specs=(anywhere, anywhere),
+        scratch_shapes=[
+            pltpu.VMEM(mixed.shape, mixed.dtype),
+            pltpu.VMEM(out.shape, out.dtype),
+            pltpu.SemaphoreType.DMA((2, 2, 4)),
+        ],
+        compiler_params=pltpu.CompilerParams(vmem_limit_bytes=58 << 20),
+    )(mixed, out)
 
 
 def on_device(hidden, queries, view_keys, view_values, ref_keys, ref_values, temporal_query, temporal_key, temporal_value):
@@ -316,15 +399,17 @@
             pltpu.VMEM((1024, 384), BF16),
             pltpu.VMEM((4, 512, 768), BF16),
             pltpu.VMEM((2, 4, 768, 1152), BF16),
-            pltpu.VMEM((3, 3, 512, 256), BF16),
+            pltpu.VMEM((2, 3, 3, 512, 256), BF16),
             pltpu.VMEM((2, 512, 384), BF16),
-            dma((3,)), dma((3, 3)), dma((3, 3)), dma((1,)), dma((1,)), dma((1,)), dma((3,)), dma((1,)), dma((1,)), dma((1,)),
-            dma((1,)), dma((4,)), dma((1,)), dma((4,)), dma((1,)), dma((1,)), dma((1,)), dma((1,)), dma((4,)),
+            dma((3,)), dma((3, 3)), dma((3, 3)), dma((1,)), dma((1,)), dma((1,)), dma((3,)), dma((2,)), dma((2,)), dma((1,)),
+            dma((1,)), dma((4,)), dma((2,)), dma((3, 4)), dma((1,)), dma((1,)), dma((1,)), dma((1,)), dma((4,)),
+            pltpu.SemaphoreType.REGULAR((1,)), pltpu.SemaphoreType.REGULAR((1,)),
         ],
         compiler_params=pltpu.CompilerParams(
             collective_id=0, has_side_effects=True, vmem_limit_bytes=58 << 20
         ),
     )(*flat, temporal_query, temporal_key, temporal_value)
+    mixed, out = copy_out(mixed, out)
     return mixed.reshape(1, 1, 128, 3072), out.reshape(1, 8, 128, 384)
 
 

time: 145 us -> 120 us (0.83)
  Pallas kernels: 140 us -> 120 us
  local copies, waits for them, and re-layouts: 4.15 us -> 0 us
    pallas_call x1, Pallas kernels: 140 us -> 117 us  [on_device(): pl.pallas_call(kernel, out_shape=(jax.ShapeDtypeStruct((128, 3072), BF16)...]
    unnamed x2 -> x0, local copies, waits for them, and re-layouts: 4.15 us -> none
    pallas_call x0 -> x1, Pallas kernels: none -> 2.29 us  [copy_out(): pl.pallas_call(copy_kernel, out_shape=(jax.ShapeDtypeStruct(mixed.shape,...]
where the time goes in v2:
time: 120 us
  Pallas kernels  120 us (100%)
    pallas_call x1, Pallas kernels, on_device(): pl.pallas_call(kernel, out_shape=(jax.ShapeDtypeStruct((128, 3072), BF16)...  117 us

profile of v2, /device:TPU:1, one launch (start us, length us, event | category | flops | bytes accessed | tf_op | source)
XLA Modules:
  0.0 120.3 jit_solution(14194369592711548846)
XLA Ops:
  0.6 117.4 %shard_map.104 = (bf16[128,3072]{1,0:T(8,128)(2,1)}, bf16[1024,384]{1,0:T(8,128)(2,1)}) custom-call(bf16[128,3072]{1,0:T(8,128)(2,1)} %bitcast.8, bf16[128,3072]{1,0:T(8,128)(2,1)} %bitcast.9, bf16[128,3072]{1,0:T(8,128)(2,1)} %bitcast.10, bf16[128,3072]{1,0:T(8,128)(2,1)} %bitcast.11, bf16[128,3072]{1,0:T(8,128)(2,1)} %bitcast.12, ...), custom_call_target="tpu_custom_call" | custom-call | tf_op jit(solution)/shard_map/pallas_call | solution.py:388
  118.0 2.3 %shard_map.105 = (bf16[128,3072]{1,0:T(8,128)(2,1)}, bf16[1024,384]{1,0:T(8,128)(2,1)}) custom-call(bf16[128,3072]{1,0:T(8,128)(2,1)} %get-tuple-element.6.mixed, bf16[1024,384]{1,0:T(8,128)(2,1)} %get-tuple-element.7.out), custom_call_target="tpu_custom_call" | custom-call | tf_op jit(solution)/shard_map/pallas_call | solution.py:371

commit v3 on v2

--- a/solution.py
+++ b/solution.py
@@ -28,7 +28,7 @@
     hid, qry, key, val, rkey, rval, wq, wk, wv,
     mixed_out, time_out,
     qbuf, kbuf, vbuf, hbuf, abuf, mbuf, xall, wbuf, tqkv, obuf,
-    p1_send, p1_recv, loc, h_send, h_recv, wl_sem, w_send, w1_recv, w2_recv, w3_recv,
+    p1_send, p1_recv, loc, h_send, h_recv, wl_sem, w_send, w1_recv, w2_recv, w3_recv, w4_recv,
     p2_send, p2_recv, p3_send, p3_recv, mb_send, mb_recv, p5_send, p5_recv, own_sem,
     core_in, plane_in,
 ):
@@ -96,36 +96,41 @@
     pl.semaphore_wait(barrier, 17)
 
     z_far = (z + 7 + 2 * zl) % 8
-
-    def part_rows(odd, p):
-        block = odd * 4 + p
-        return column(block), wbuf.at[1, p, pl.ds(pl.multiple_of(odd * 384, 384), 384)]
-
-    odd = y % 2
-
-    def bring(n):
-        rows, place = part_rows(odd, 2 * n + c)
-        for a, w in enumerate((wq, wk, wv)):
-            remote(
-                w.at[rows],
-                place.at[:, a * 384 : (a + 1) * 384],
-                w_send.at[0],
-                w1_recv.at[n],
-                device(y, z_far, c, x),
-            ).start()
-
-    def part_wait(sem):
-        bytes_wait(wbuf.at[1, 0, 0:384], sem)
-
-    def to_y(n):
-        _, place = part_rows(odd, 2 * n + c)
-        remote(place, place, w_send.at[1], w2_recv.at[n], device((y + 1 + 2 * n) % 4, z, c, x)).start()
-
-    def to_core(set_odd, n):
-        _, place = part_rows(set_odd, 2 * n + c)
+    part_at = pl.ds(pl.multiple_of(c * 384, 384), 384)
+
+    def piece(y_, a):
+        return wbuf.at[1, y_, part_at, a * 384 : (a + 1) * 384]
+
+    def bring(a):
+        source = (wq, wk, wv)[a].at[column(c * 4 + y)]
+        remote(source, piece(y, a), w_send.at[0], w1_recv.at[a], device(y, z_far, c, x)).start()
+
+    def to_core(y_, a):
+        place = piece(y_, a)
         remote(place, place, w_send.at[2], w3_recv.at[0], device(y, z, 1 - c, x)).start()
 
-    bring(0)
+    def pass_on(a):
+        place = piece(y, a)
+        bytes_wait(place, w1_recv.at[a])
+        for n in range(2):
+            remote(place, place, w_send.at[1], w2_recv.at[n, a], device((y + 1 + 2 * n) % 4, z, c, x)).start()
+        to_core(y, a)
+
+    def pass_far(a):
+        for n in range(2):
+            from_y = (y + 3 + 2 * n) % 4
+            bytes_wait(piece(y, a), w2_recv.at[n, a])
+            rows = pl.ds(pl.multiple_of(c * 384 + n * 192, 192), 192)
+            place = wbuf.at[1, from_y, rows, a * 384 : (a + 1) * 384]
+            remote(place, place, w_send.at[1], w4_recv.at[a], device((y + 1 + 2 * n) % 4, z, c, x)).start()
+            to_core(from_y, a)
+
+    def pass_last(a):
+        bytes_wait(piece(y, a), w4_recv.at[a])
+        to_core((y + 2) % 4, a)
+
+    for a in range(3):
+        bring(a)
 
     def send_heads(h, _):
         def to(i, _):
@@ -171,56 +176,53 @@
 
         return lax.fori_loop(0, 4, rows, 0)
 
-    lax.fori_loop(0, 1, view_head, 0)
-    bring(1)
     pl.semaphore_wait(core_in.at[0], 1)
     for i in range(1, 4):
         greet(device((y + i) % 4, z, c, x), plane_in.at[0])
+    pass_on(0)
+    lax.fori_loop(0, 1, view_head, 0)
+    pass_on(1)
     lax.fori_loop(1, 2, view_head, 0)
-    part_wait(w1_recv.at[0])
-    to_y(0)
-    to_core(odd, 0)
+    pass_on(2)
+    pass_far(0)
     lax.fori_loop(2, 3, view_head, 0)
+    pass_far(1)
+    pass_far(2)
     pl.semaphore_wait(plane_in.at[0], 3)
 
     bytes_wait(hbuf.at[0:1], own_sem.at[0])
     bytes_wait(hbuf.at[0:7], h_recv.at[0])
 
+    def residual(i, _):
+        views = pl.ds(i * 2, 2)
+        block = hbuf[views].astype(F32) + jnp.concatenate([abuf[h, views] for h in range(3)], axis=-1)
+        mbuf[pl.ds(pl.multiple_of(i * 256, 256), 256)] = block.reshape(256, 384).astype(BF16)
+        return 0
+
+    lax.fori_loop(0, 4, residual, 0)
+
     def tokens_out(n, _):
-        c_to, d = n // 4, n % 4
+        d = n
         y_to = (y + d) % 4
 
-        @pl.when(c_to == 0)
-        def _():
-            views = pl.ds(y_to * 2, 2)
-            block = hbuf[views].astype(F32) + jnp.concatenate([abuf[h, views] for h in range(3)], axis=-1)
-            mbuf[pl.ds(pl.multiple_of(y_to * 256, 256), 256)] = block.reshape(256, 384).astype(BF16)
-
         def to(j, _):
-            z_to = (z + j) % 8
+            z_to, c_to = (z + j // 2) % 8, (c + j % 2) % 2
             group = y_to * 16 + z_to * 2 + c_to
-            remote(
-                mbuf.at[pl.ds(pl.multiple_of(group * 16, 16), 16)],
-                xall.at[x, pl.ds(pl.multiple_of(d * 128 + (f % 8) * 16, 16), 16), column(zl)],
-                p2_send.at[0],
-                p2_recv.at[d],
-                device(y_to, z_to, c_to, x),
-            ).start()
+            source = mbuf.at[pl.ds(pl.multiple_of(group * 16, 16), 16)]
+            place = xall.at[x, pl.ds(pl.multiple_of(d * 128 + (f % 8) * 16, 16), 16), column(zl)]
+            here = (d == 0) & (j == 0)
+
+            @pl.when(here)
+            def _():
+                pltpu.make_async_copy(source, place, p2_recv.at[0]).start()
+
+            @pl.when(jnp.logical_not(here))
+            def _():
+                remote(source, place, p2_send.at[0], p2_recv.at[d], device(y_to, z_to, c_to, x)).start()
+
             return 0
 
-        return lax.fori_loop(jnp.where((d == 0) & (c_to == c), 1, 0), 8, to, 0)
-
-    lax.fori_loop(0, 8, tokens_out, 0)
-    mine = pltpu.make_async_copy(
-        mbuf.at[pl.ds(pl.multiple_of((y * 16 + z * 2 + c) * 16, 16), 16)],
-        xall.at[x, pl.ds(pl.multiple_of((f % 8) * 16, 16), 16), column(zl)],
-        own_sem.at[1],
-    )
-    mine.start()
-    mine_mixed = pltpu.make_async_copy(
-        mbuf.at[pl.ds(pl.multiple_of(v * 128, 128), 128)], mixed_out.at[:, column(v)], own_sem.at[2]
-    )
-    mine_mixed.start()
+        return lax.fori_loop(0, 16, to, 0)
 
     def send_mixed(i, _):
         w = (zl + i // 4) % 2 * 4 + (x + i % 4) % 4
@@ -233,11 +235,6 @@
         ).start()
         return 0
 
-    lax.fori_loop(1, 4, send_mixed, 0)
-    part_wait(w1_recv.at[1])
-    to_y(1)
-    to_core(odd, 1)
-
     def x_device(i):
         return (f, zl * 4 + (x + i) % 4)
 
@@ -253,19 +250,32 @@
             block = xall.at[(x + 3 + 2 * n) % 4, rows]
             remote(block, block, p3_send.at[1], p3_recv.at[2, d], x_device(1 + 2 * n)).start()
 
-    def gather(d, _):
-        bytes_wait(mbuf.at[0:256], p2_recv.at[d])
-        direct(d)
-        forward(d - 1)
-        return 0
-
-    mine.wait()
-    bytes_wait(mbuf.at[0:240], p2_recv.at[0])
-    direct(0)
-    lax.fori_loop(1, 2, gather, 0)
-    part_wait(w2_recv.at[0])
-    to_core(1 - odd, 0)
-    lax.fori_loop(2, 4, gather, 0)
+    def step(t, _):
+        @pl.when(t < 4)
+        def _():
+            tokens_out(t, 0)
+
+        @pl.when(t == 0)
+        def _():
+            lax.fori_loop(1, 4, send_mixed, 0)
+
+        @pl.when(t >= 1)
+        def _():
+            bytes_wait(mbuf.at[0:256], p2_recv.at[t - 1])
+            direct(t - 1)
+
+        @pl.when(t >= 2)
+        def _():
+            forward(t - 2)
+
+        return 0
+
+    lax.fori_loop(0, 5, step, 0)
+    mine_mixed = pltpu.make_async_copy(
+        mbuf.at[pl.ds(pl.multiple_of(v * 128, 128), 128)], mixed_out.at[:, column(v)], own_sem.at[2]
+    )
+    mine_mixed.start()
+
     bytes_wait(wbuf.at[0], wl_sem.at[0])
 
     row = lax.broadcasted_iota(jnp.int32, (1, 16, 512), 1)
@@ -296,10 +306,10 @@
         bytes_wait(xall.at[0, 0:128], p3_recv.at[2, d])
     project(0, 0)
     forward(3)
-    part_wait(w2_recv.at[1])
-    to_core(1 - odd, 1)
+    for a in range(3):
+        pass_last(a)
+    bytes_wait(wbuf.at[1, :, 0:384], w3_recv.at[0])
     lax.fori_loop(4, 8, send_mixed, 0)
-    bytes_wait(wbuf.at[1, :, 0:384], w3_recv.at[0])
     project(1, 0)
     for d in range(2, 4):
         bytes_wait(xall.at[0, 0:128], p3_recv.at[2, d])
@@ -335,8 +345,8 @@
     for a in range(3):
         bytes_wait(kbuf.at[:, 0:7], p1_send.at[a])
     bytes_wait(hbuf.at[0:7], h_send.at[0])
-    bytes_wait(wbuf.at[1, 0:2, 0:384], w_send.at[0])
-    bytes_wait(wbuf.at[1, 0:2, 0:384], w_send.at[1])
+    bytes_wait(wbuf.at[1, 0, 0:384], w_send.at[0])
+    bytes_wait(wbuf.at[1, 0:3, 0:384], w_send.at[1])
     bytes_wait(wbuf.at[1, :, 0:384], w_send.at[2])
     bytes_wait(mbuf.at[0:1008], p2_send.at[0])
     bytes_wait(xall.at[0:2], p3_send.at[0])
@@ -401,8 +411,8 @@
             pltpu.VMEM((2, 4, 768, 1152), BF16),
             pltpu.VMEM((2, 3, 3, 512, 256), BF16),
             pltpu.VMEM((2, 512, 384), BF16),
-            dma((3,)), dma((3, 3)), dma((3, 3)), dma((1,)), dma((1,)), dma((1,)), dma((3,)), dma((2,)), dma((2,)), dma((1,)),
-            dma((1,)), dma((4,)), dma((2,)), dma((3, 4)), dma((1,)), dma((1,)), dma((1,)), dma((1,)), dma((4,)),
+            dma((3,)), dma((3, 3)), dma((3, 3)), dma((1,)), dma((1,)), dma((1,)), dma((3,)), dma((3,)), dma((2, 3)), dma((1,)), dma((3,)),
+            dma((2,)), dma((4,)), dma((2,)), dma((3, 4)), dma((1,)), dma((1,)), dma((1,)), dma((1,)), dma((4,)),
             pltpu.SemaphoreType.REGULAR((1,)), pltpu.SemaphoreType.REGULAR((1,)),
         ],
         compiler_params=pltpu.CompilerParams(

time: 120 us -> 113 us (0.942)
  Pallas kernels: 120 us -> 113 us
    pallas_call x1, Pallas kernels: 117 us -> 110 us  [on_device(): pl.pallas_call(kernel, out_shape=(jax.ShapeDtypeStruct((128, 3072), BF16)...]
where the time goes in v3:
time: 113 us
  Pallas kernels  113 us (100%)
    pallas_call x1, Pallas kernels, on_device(): pl.pallas_call(kernel, out_shape=(jax.ShapeDtypeStruct((128, 3072), BF16)...  110 us
    pallas_call x1, Pallas kernels, copy_out(): pl.pallas_call(copy_kernel, out_shape=(jax.ShapeDtypeStruct(mixed.shape,...  2.29 us

profile of v3, /device:TPU:1, one launch (start us, length us, event | category | flops | bytes accessed | tf_op | source)
XLA Modules:
  0.0 113.2 jit_solution(9301131048798685531)
XLA Ops:
  0.6 110.2 %shard_map.104 = (bf16[128,3072]{1,0:T(8,128)(2,1)}, bf16[1024,384]{1,0:T(8,128)(2,1)}) custom-call(bf16[128,3072]{1,0:T(8,128)(2,1)} %bitcast.8, bf16[128,3072]{1,0:T(8,128)(2,1)} %bitcast.9, bf16[128,3072]{1,0:T(8,128)(2,1)} %bitcast.10, bf16[128,3072]{1,0:T(8,128)(2,1)} %bitcast.11, bf16[128,3072]{1,0:T(8,128)(2,1)} %bitcast.12, ...), custom_call_target="tpu_custom_call" | custom-call | tf_op jit(solution)/shard_map/pallas_call | solution.py:398
  110.9 2.3 %shard_map.105 = (bf16[128,3072]{1,0:T(8,128)(2,1)}, bf16[1024,384]{1,0:T(8,128)(2,1)}) custom-call(bf16[128,3072]{1,0:T(8,128)(2,1)} %get-tuple-element.6.mixed, bf16[1024,384]{1,0:T(8,128)(2,1)} %get-tuple-element.7.out), custom_call_target="tpu_custom_call" | custom-call | tf_op jit(solution)/shard_map/pallas_call | solution.py:381

commit v4 on v3

--- a/solution.py
+++ b/solution.py
@@ -206,7 +206,9 @@
         y_to = (y + d) % 4
 
         def to(j, _):
-            z_to, c_to = (z + j // 2) % 8, (c + j % 2) % 2
+            m = j // 2
+            z_to = (z + jnp.where(m % 2 == 1, (m + 1) // 2, 8 - m // 2)) % 8
+            c_to = (c + j % 2) % 2
             group = y_to * 16 + z_to * 2 + c_to
             source = mbuf.at[pl.ds(pl.multiple_of(group * 16, 16), 16)]
             place = xall.at[x, pl.ds(pl.multiple_of(d * 128 + (f % 8) * 16, 16), 16), column(zl)]
@@ -320,7 +322,9 @@
         zl_to = (zl + s) % 2
 
         def to(i, _):
-            f_to = (f + i) % 32
+            n = (i // 2) % 4
+            n = jnp.where(n >= 2, 5 - n, n)
+            f_to = (y + i // 8) % 4 * 8 + (zh + n) % 4 * 2 + (c + i % 2) % 2
             remote(
                 obuf.at[s, pl.ds(pl.multiple_of((y + 4 - f_to // 8) % 4 * 128 + (f_to % 8) * 16, 16), 16)],
                 time_out.at[group_rows],

time: 113 us -> 114 us (level)
    pallas_call x1, Pallas kernels: 110 us -> 111 us  [on_device(): pl.pallas_call(kernel, out_shape=(jax.ShapeDtypeStruct((128, 3072), BF16)...]
where the time goes in v4:
time: 114 us
  Pallas kernels  114 us (100%)
    pallas_call x1, Pallas kernels, on_device(): pl.pallas_call(kernel, out_shape=(jax.ShapeDtypeStruct((128, 3072), BF16)...  111 us
    pallas_call x1, Pallas kernels, copy_out(): pl.pallas_call(copy_kernel, out_shape=(jax.ShapeDtypeStruct(mixed.shape,...  2.29 us

profile of v4, /device:TPU:1, one launch (start us, length us, event | category | flops | bytes accessed | tf_op | source)
XLA Modules:
  0.0 114.4 jit_solution(1080862678528016105)
XLA Ops:
  0.6 111.4 %shard_map.104 = (bf16[128,3072]{1,0:T(8,128)(2,1)}, bf16[1024,384]{1,0:T(8,128)(2,1)}) custom-call(bf16[128,3072]{1,0:T(8,128)(2,1)} %bitcast.8, bf16[128,3072]{1,0:T(8,128)(2,1)} %bitcast.9, bf16[128,3072]{1,0:T(8,128)(2,1)} %bitcast.10, bf16[128,3072]{1,0:T(8,128)(2,1)} %bitcast.11, bf16[128,3072]{1,0:T(8,128)(2,1)} %bitcast.12, ...), custom_call_target="tpu_custom_call" | custom-call | tf_op jit(solution)/shard_map/pallas_call | solution.py:402
  112.1 2.3 %shard_map.105 = (bf16[128,3072]{1,0:T(8,128)(2,1)}, bf16[1024,384]{1,0:T(8,128)(2,1)}) custom-call(bf16[128,3072]{1,0:T(8,128)(2,1)} %get-tuple-element.6.mixed, bf16[1024,384]{1,0:T(8,128)(2,1)} %get-tuple-element.7.out), custom_call_target="tpu_custom_call" | custom-call | tf_op jit(solution)/shard_map/pallas_call | solution.py:385
